TPU v7x, 32 devices: a whole 2x2x4 slice. The times are simulated.
32 devices in a mesh: blk: 8 (over z, core), batch: 2 (over x), tensor: 2 (over y).
Axes of the slice: x: 2, y: 2, z: 4, core: 2. Of those that a mesh axis runs over, the one named last changes fastest.
Arguments:
- queries: bfloat16 [64, 8192], P(('blk', 'batch'), 'tensor'), may hold values from -32 to 32
- new_keys: bfloat16 [64, 1024], P(('blk', 'batch'), 'tensor'), may hold values from -15 to 15
- new_values: bfloat16 [64, 1024], P(('blk', 'batch'), 'tensor'), may hold values from -6 to 6
- suffix_keys: bfloat16 [64, 512, 1024], P(('blk', 'batch'), None, 'tensor'), may hold values from -9 to 9
- suffix_values: bfloat16 [64, 512, 1024], P(('blk', 'batch'), None, 'tensor'), may hold values from -6 to 6
- suffix_lengths: int32 [64], P(('blk', 'batch')), may hold values from 0 to 512, as said below
- prefix_keys: bfloat16 [16384, 1024], P('blk', 'tensor'), may hold values from -6 to 6
- prefix_values: bfloat16 [16384, 1024], P('blk', 'tensor'), may hold values from -6 to 6
- out_weight: bfloat16 [8192, 4096], P('tensor', 'batch'), may hold values from -0.0625 to 0.0625
Outputs:
- projected: bfloat16 [64, 4096], P(('blk', 'tensor'), 'batch')
Inputs may be any that keep to these rules, and one draw needn't show every extreme that they name: `suffix_lengths`: some sample has exactly 512 live slots.
All inputs are finite; a program needn't handle non-finite values.
Results may differ from a plain program's by a relative error of at most 0.005.
Values may be sent and summed in bfloat16 or wider, within the bound.
A program may use at most 128 MiB of HBM per device.

v0:
```python
import jax
import jax.numpy as jnp
from jax import lax
from jax.sharding import PartitionSpec as P

HD = 128


def split_heads(rows_array, kv_count):
    return rows_array.reshape(rows_array.shape[0], kv_count, -1, HD)


def group_scores(query_rows, key_rows):
    kv_count = key_rows.shape[-1] // HD
    query_heads = split_heads(query_rows, kv_count)
    key_heads = key_rows.reshape(key_rows.shape[0], kv_count, HD)
    return jnp.einsum(
        "nkgd,pkd->nkgp", query_heads, key_heads, preferred_element_type=jnp.float32
    ) * HD ** (-0.5)


def row_maximum(scores):
    return scores.max(-1).reshape(scores.shape[0], -1)


def group_sums(scores, row_top, value_rows):
    row_count = scores.shape[0]
    kv_count = scores.shape[1]
    weights = jnp.exp(scores - row_top.reshape(row_count, kv_count, -1)[..., None]).astype(
        jnp.bfloat16
    )
    row_mass = jnp.sum(lax.optimization_barrier(weights).astype(jnp.float32), axis=-1).reshape(
        row_count, -1
    )
    value_heads = value_rows.reshape(value_rows.shape[0], kv_count, HD)
    weighted = jnp.einsum(
        "nkgp,pkd->nkgd", weights, value_heads, preferred_element_type=jnp.float32
    )
    return (weighted.reshape(row_count, -1), row_mass)


def rescale_rows(weighted, row_mass, scale):
    row_count = weighted.shape[0]
    scaled = weighted.reshape(row_count, scale.shape[1], -1) * scale[..., None]
    return (scaled.reshape(row_count, -1), row_mass * scale)


def masked_block(query_heads, key_block, lengths):
    block_scores = jnp.einsum(
        "nkgd,ntkd->nkgt", query_heads, key_block, preferred_element_type=jnp.float32
    ) * HD ** (-0.5)
    slot_index = lax.iota(jnp.int32, key_block.shape[1])
    live_slots = slot_index[None, :] < lengths[:, None]
    return jnp.where(live_slots[:, None, None, :], block_scores, -jnp.inf)


def body(
    queries,
    new_keys,
    new_values,
    suffix_keys,
    suffix_values,
    suffix_lengths,
    prefix_keys,
    prefix_values,
    out_weight,
):
    row_count = queries.shape[0]
    kv_count = new_keys.shape[-1] // HD
    slots = suffix_keys.shape[1]
    query_heads = split_heads(queries, kv_count)
    suffix_key_heads = suffix_keys.reshape(row_count, slots, kv_count, HD)
    suffix_value_heads = suffix_values.reshape(row_count, slots, kv_count, HD)
    own_scores = jnp.einsum(
        "nkgd,nkd->nkg",
        query_heads,
        new_keys.reshape(row_count, kv_count, HD),
        preferred_element_type=jnp.float32,
    ) * HD ** (-0.5)
    suffix_scores = masked_block(query_heads, suffix_key_heads, suffix_lengths)
    local_top = jnp.maximum(suffix_scores.max(-1), own_scores)
    local_top_rows = local_top.reshape(row_count, -1)
    gathered = lax.all_gather(queries, "blk", axis=0, tiled=True)
    scores = group_scores(gathered, prefix_keys)
    own_start = lax.axis_index("blk") * row_count
    piece_top = row_maximum(scores)
    own_top = lax.dynamic_slice_in_dim(piece_top, own_start, row_count, 0)
    joined_top = lax.dynamic_update_slice_in_dim(
        piece_top, jnp.maximum(own_top, local_top_rows), own_start, 0
    )
    full_top = lax.pmax(joined_top, "blk")
    weighted, row_mass = group_sums(scores, piece_top, prefix_values)
    weighted, row_mass = rescale_rows(weighted, row_mass, jnp.exp(piece_top - full_top))
    weighted, row_mass = (
        lax.psum_scatter(weighted, "blk", scatter_dimension=0, tiled=True),
        lax.psum_scatter(row_mass, "blk", scatter_dimension=0, tiled=True),
    )
    row_top = lax.dynamic_slice_in_dim(full_top, own_start, row_count, 0)
    top_heads = row_top.reshape(row_count, kv_count, -1)
    weighted_heads = weighted.reshape(row_count, kv_count, -1, HD)
    mass_heads = row_mass.reshape(row_count, kv_count, -1)
    own_weights = jnp.exp(own_scores - top_heads).astype(jnp.bfloat16)
    own_float = lax.optimization_barrier(own_weights).astype(jnp.float32)
    mass_heads = mass_heads + own_float
    weighted_heads = weighted_heads + own_float[..., None] * new_values.reshape(
        row_count, kv_count, 1, HD
    ).astype(jnp.float32)
    suffix_weights = jnp.exp(suffix_scores - top_heads[..., None]).astype(jnp.bfloat16)
    mass_heads = mass_heads + jnp.sum(
        lax.optimization_barrier(suffix_weights).astype(jnp.float32), axis=-1
    )
    weighted_heads = weighted_heads + jnp.einsum(
        "nkgt,ntkd->nkgd", suffix_weights, suffix_value_heads, preferred_element_type=jnp.float32
    )
    attended = (weighted_heads / mass_heads[..., None]).reshape(row_count, -1).astype(jnp.bfloat16)
    projected = jnp.dot(
        lax.all_gather(attended, "batch", axis=0, tiled=True),
        out_weight,
        preferred_element_type=jnp.float32,
    )
    return lax.psum_scatter(projected, "tensor", scatter_dimension=0, tiled=True).astype(
        jnp.bfloat16
    )


def solution(mesh):
    in_specs = (
        P(("blk", "batch"), "tensor"),
        P(("blk", "batch"), "tensor"),
        P(("blk", "batch"), "tensor"),
        P(("blk", "batch"), None, "tensor"),
        P(("blk", "batch"), None, "tensor"),
        P(("blk", "batch")),
        P("blk", "tensor"),
        P("blk", "tensor"),
        P("tensor", "batch"),
    )
    out_specs = P(("blk", "tensor"), "batch")
    return jax.shard_map(body, mesh=mesh, in_specs=in_specs, out_specs=out_specs, check_vma=False)
```

profile of v0, /device:TPU:0, one launch (start us, length us, event | category | flops | bytes accessed | tf_op | source)
XLA Modules:
  0.0 166.3 jit_solution(18334106535279688546)
XLA Ops:
  6.5 0.0 copy-start
  6.5 0.0 all-reduce.5.cloned.1.call-start
  6.5 0.0 copy-start.3
  6.6 4.2 %reshape.76 = bf16[2048,4,128]{2,1,0:T(4,128)(2,1)} reshape(bf16[2048,512]{1,0:T(8,128)(2,1)} %param.15) | data formatting | bytes 4194304 | tf_op jit(solution)/shard_map/reshape | solution.py:16
  10.7 0.0 copy-done.2
  10.7 15.9 %all-gather = bf16[8,4,4096]{2,1,0:T(4,128)(2,1)S(1)} all-gather(bf16[1,4,4096]{2,1,0:T(4,128)(2,1)S(1)} %bitcast.95), channel_id=1, replica_groups=mesh['blk'=8,'batch'=2,'tensor'=2] {'blk'}, dimensions={0}, use_global_device_ids=true | all-gather | bytes 294912 | tf_op jit(solution)/shard_map/all_gather | solution.py:83
  26.6 0.3 reshape.77
  26.9 0.0 copy-done.5
  26.9 0.1 iota_compare_fusion
  27.0 0.0 copy-done.3
  27.0 0.1 fusion.31
  27.1 0.7 fusion.36
  27.9 0.1 copy.45
  28.0 6.1 %bitcast_reduce_fusion = (f32[32,4,8]{0,2,1:T(8,128)S(1)}, f32[4,2048,32,8]{1,2,3,0:T(8,128)}) fusion(bf16[32,4,8,128]{3,2,1,0:T(8,128)(2,1)S(1)} %reshape.77, bf16[2048,4,128,1]{2,1,0,3:T(4,128)(2,1)} %bitcast.89), kind=kOutput, calls=%fused_computation.1 | convolution fusion | flops 541064192 | bytes 10752000 | tf_op jit(solution)/shard_map/nkgd,pkd->nkgp/dot_general | solution.py:17
  34.1 0.1 bitcast_maximum_fusion
  34.1 0.2 dynamic_update_slice.3
  34.3 29.2 %pmax.7 = f32[32,32]{0,1:T(8,128)S(1)} all-reduce(f32[32,32]{0,1:T(8,128)S(1)} %dynamic_update_slice.3), channel_id=1, replica_groups=mesh['blk'=8,'batch'=2,'tensor'=2] {'blk'}, use_global_device_ids=true, to_apply=%region_2.3 | all-reduce | flops 1024 | bytes 8192 | tf_op jit(solution)/shard_map/pmax | solution.py:91
  63.6 4.2 %fusion.1 = bf16[32,4,8,2048]{3,0,2,1:T(8,128)(2,1)S(1)} fusion(f32[4,2048,32,8]{1,2,3,0:T(8,128)} %get-tuple-element.8, f32[32,4,8]{0,2,1:T(8,128)S(1)} %get-tuple-element.7), kind=kLoop, calls=%fused_computation.3 | loop fusion | flops 6291456 | bytes 12587008 | tf_op jit(solution)/shard_map/convert_element_type | solution.py:29
  67.7 0.0 copy-start.1
  67.7 0.6 convert_reduce_fusion
  68.4 1.3 copy-done.1
  69.7 0.1 copy.33
  69.7 4.0 %reshape.78 = bf16[2048,4,128]{2,1,0:T(4,128)(2,1)} reshape(bf16[2048,512]{1,0:T(8,128)(2,1)} %param.16) | data formatting | bytes 4194304 | tf_op jit(solution)/shard_map/reshape | solution.py:35
  73.7 4.2 %fusion.12 = f32[32,4,8,128]{3,0,2,1:T(8,128)S(1)} fusion(bf16[32,4,8,2048]{3,0,2,1:T(8,128)(2,1)} %copy-done.1, bf16[2048,4,128,1]{2,1,0,3:T(4,128)(2,1)} %bitcast.92), kind=kOutput, calls=%fused_computation.15 | convolution fusion | flops 536870912 | bytes 6815744 | tf_op jit(solution)/shard_map/nkgp,pkd->nkgd/dot_general | solution.py:36
  77.9 0.0 copy-start.7
  77.9 0.0 copy-start.4
  77.9 0.0 copy-start.6
  77.9 0.3 copy.30
  78.3 0.2 mul.59
  78.5 1.4 bitcast_multiply_fusion
  79.9 0.0 all-reduce.5.cloned.1.call-update
  79.9 0.1 dynamic-slice_bitcast_fusion.2
  80.0 0.1 copy.46
  80.1 0.1 exponential_convert_fusion
  80.2 0.1 convert_reduce_fusion.1
  80.3 26.0 %all-reduce.1 = f32[32,32]{0,1:T(8,128)S(1)} all-reduce(f32[32,32]{0,1:T(8,128)S(1)} %get-tuple-element.5), channel_id=3, replica_groups=mesh['blk'=8,'batch'=2,'tensor'=2] {'blk'}, use_global_device_ids=true, to_apply=%region_5.6.clone | all-reduce | flops 1024 | bytes 8192
  106.3 0.6 dynamic-slice
  107.5 0.1 dynamic-slice_bitcast_fusion.1
  107.6 0.1 copy.47
  107.7 0.0 copy-done.6
  107.7 0.6 dynamic-slice.4
  109.0 25.5 %all-reduce.5.cloned.1.call-done = f32[32,4096]{1,0:T(8,128)} async-done(((f32[32,4096]{1,0:T(8,128)}), f32[32,4096]{1,0:T(8,128)}) %all-reduce.5.cloned.1.call-update) | async-done | bytes 524304
  134.4 0.9 dynamic-slice_bitcast_fusion
  135.4 2.0 %fusion.27 = bf16[4,4,8,128]{3,2,1,0:T(8,128)(2,1)S(1)} fusion(bf16[4,4,8,512]{3,2,1,0:T(8,128)(2,1)S(1)} %exponential_convert_fusion, f32[1,4,32,128]{3,1,2,0:T(4,128)S(1)} %dynamic-slice_bitcast_fusion, f32[4,4,8]{2,1,0:T(4,128)S(1)} %bitcast.103, f32[4,4,128]{2,1,0:T(4,128)S(1)} %reshape.89, f32[4,4,8]{2,1,0:T(4,128)S(1)} %convert_element_type.40, ...), kind=kOutput, calls=%fused_computation.20 | convolution fusion | flops 16859136 | bytes 2335744 | tf_op jit(solution)/shard_map/nkgt,ntkd->nkgd/dot_general | solution.py:112
  137.4 4.6 %all-gather.1 = bf16[2,4,4096]{2,1,0:T(4,128)(2,1)S(1)} all-gather(bf16[1,4,4096]{2,1,0:T(4,128)(2,1)S(1)} %reshape.92), channel_id=1, replica_groups=mesh['blk'=8,'batch'=2,'tensor'=2] {'batch'}, dimensions={0}, use_global_device_ids=true | all-gather | bytes 98304 | tf_op jit(solution)/shard_map/all_gather | solution.py:117
  142.0 8.0 %fusion.37 = f32[8,2048]{1,0:T(8,128)S(1)} fusion(bf16[8,4096]{1,0:T(8,128)(2,1)S(1)} %reshape.93, bf16[4096,2048]{1,0:T(8,128)(2,1)} %param.17), kind=kOutput, calls=%fused_computation.43 | convolution fusion | flops 134217728 | bytes 16908288 | tf_op jit(solution)/shard_map/dot_general | solution.py:116
  150.0 8.8 %all-reduce.2 = bf16[8,2048]{1,0:T(8,128)(2,1)S(1)} all-reduce(f32[8,2048]{1,0:T(8,128)S(1)} %fusion.37), channel_id=4, replica_groups=mesh['blk'=8,'batch'=2,'tensor'=2] {'tensor'}, use_global_device_ids=true, to_apply=%region_7.8.clone | all-reduce | flops 16384 | bytes 98304
  158.9 0.6 dynamic-slice_convert_fusion
  (15 shorter events, 0.1 us)
Async XLA Ops:
  6.5 20.6 %copy-start = (bf16[4,512,512]{2,1,0:T(8,128)(2,1)S(1)}, bf16[4,512,512]{2,1,0:T(8,128)(2,1)}, u32[]{:S(2)}) copy-start(bf16[4,512,512]{2,1,0:T(8,128)(2,1)} %param.12) | copy-start | bytes 6291460
  6.5 127.9 %all-reduce.5.cloned.1.call-start = ((), (), s32[]{:S(2)}) async-start(), calls=%async_computation | async-start | bytes 1048576
  6.5 4.2 %copy-start.2 = (bf16[4,4096]{1,0:T(4,128)(2,1)S(1)}, bf16[4,4096]{1,0:T(4,128)(2,1)}, u32[]{:S(2)}) copy-start(bf16[4,4096]{1,0:T(4,128)(2,1)} %param.9) | copy-start | bytes 98308
  6.5 20.3 %copy-start.5 = (s32[4]{0:T(128)S(1)}, s32[4]{0:T(128)}, u32[]{:S(2)}) copy-start(s32[4]{0:T(128)} %param.14) | copy-start | bytes 52
  6.5 20.4 %copy-start.3 = (bf16[4,512]{1,0:T(4,128)(2,1)S(1)}, bf16[4,512]{1,0:T(4,128)(2,1)}, u32[]{:S(2)}) copy-start(bf16[4,512]{1,0:T(4,128)(2,1)} %param.10) | copy-start | bytes 12292
  67.7 1.9 %copy-start.1 = (bf16[32,4,8,2048]{3,0,2,1:T(8,128)(2,1)}, bf16[32,4,8,2048]{3,0,2,1:T(8,128)(2,1)S(1)}, u32[]{:S(2)}) copy-start(bf16[32,4,8,2048]{3,0,2,1:T(8,128)(2,1)S(1)} %fusion.1) | copy-start | bytes 12582916
  77.9 28.4 %copy-start.7 = (u32[32]{0:T(128)S(1)}, u32[32]{0:T(128)}, u32[]{:S(2)}) copy-start(u32[32]{0:T(128)} %constant.28) | copy-start | bytes 388
  77.9 29.8 %copy-start.4 = (bf16[4,512]{1,0:T(4,128)(2,1)S(1)}, bf16[4,512]{1,0:T(4,128)(2,1)}, u32[]{:S(2)}) copy-start(bf16[4,512]{1,0:T(4,128)(2,1)} %param.11) | copy-start | bytes 12292
  77.9 29.8 %copy-start.6 = (u32[32]{0:T(128)S(1)}, u32[32]{0:T(128)}, u32[]{:S(2)}) copy-start(u32[32]{0:T(128)} %constant.36) | copy-start | bytes 388
Sparse Core Ops, SparseCore 0:
  80.0 54.3 all-reduce.4
where the time goes:
time: 167 us; the launch traced here: 166 us
  blocking collectives  84.5 us (51%)
  waiting for transfers between devices  25.5 us (15%)
  matrix products  21.2 us (13%)
  between operations  14.8 us (9%)
  local copies, waits for them, and re-layouts  13.7 us (8%)
  other arithmetic  6.6 us (4%)
    unnamed x2, blocking collectives  34.8 us
    pmax x1, blocking collectives, body(): full_top = lax.pmax(joined_top, 'blk')  29.2 us
    unnamed x2, waiting for transfers between devices  25.5 us
    all_gather x1, blocking collectives, body(): gathered = lax.all_gather(queries, 'blk', axis=0, tiled=True)  15.9 us
    dot_general x1, matrix products, body(): jnp.dot(lax.all_gather(attended, 'batch', axis=0, tiled=True), out_weight...  8.04 us
    dot_general x1, matrix products, group_scores(): jnp.einsum('nkgd,pkd->nkgp', query_heads, key_heads, preferred_element_ty...  6.1 us
    all_gather x1, blocking collectives, body(): lax.all_gather(attended, 'batch', axis=0, tiled=True)  4.59 us
    dot_general x1, matrix products, group_sums(): jnp.einsum('nkgp,pkd->nkgd', weights, value_heads, preferred_element_type...  4.19 us
  transfers between devices with their start and end apart: 1, of which 1 were waited for; matrix products, arithmetic and copies ran while one was open for 1% of the time, Pallas kernels for 0%

commit v1 on v0

v1 whole, which is shorter than its diff:
```python
import functools

import jax
import jax.numpy as jnp
from jax import lax
from jax.experimental import pallas as pl
from jax.experimental.pallas import tpu as pltpu
from jax.sharding import PartitionSpec as P

HD = 128
SCALE = HD ** (-0.5)
F32 = jnp.float32
BF16 = jnp.bfloat16
MESH = pl.DeviceIdType.MESH
NT = (((1,), (1,)), ((), ()))
KEY_CHUNK = 512
COL_CHUNK = 256


def head_lanes(k):
    return pl.ds(pl.multiple_of(k * HD, HD), HD)


def kernel(
    nb, nbt, nt, n,
    q_ref, nk_ref, nv_ref, len_ref, sk_hbm, sv_hbm, pk_hbm, pv_hbm, w_hbm,
    o_ref,
    sk, sv, pk, pv, w, qbuf, sbuf, stat, psend, prec, lacc, lm, lmass,
    abuf, a32, x, osend, orecv,
    lsem, q_s, q_r, p_s, p_r, a_s, a_r, o_s, o_r,
):
    kv, rows, _ = q_ref.shape
    groups = rows // n
    slots = sk.shape[1]
    prefix = pk.shape[0]
    me = lax.axis_index("blk")
    mb = lax.axis_index("batch")
    mt = lax.axis_index("tensor")

    loads = [
        pltpu.make_async_copy(src, dst, lsem.at[i])
        for i, (src, dst) in enumerate(
            [(sk_hbm, sk), (sv_hbm, sv), (pk_hbm, pk), (pv_hbm, pv), (w_hbm, w)]
        )
    ]
    for load in loads:
        load.start()

    barrier = pltpu.get_barrier_semaphore()
    for axis, mine, size in (("blk", me, nb), ("batch", mb, nbt), ("tensor", mt, nt)):
        for r in range(1, size):
            pl.semaphore_signal(
                barrier, inc=1, device_id={axis: lax.rem(mine + r, size)}, device_id_type=MESH
            )
    qbuf[:, me] = q_ref[...]
    pl.semaphore_wait(barrier, nb + nbt + nt - 3)

    def q_copy(k, r):
        return pltpu.make_async_remote_copy(
            src_ref=q_ref.at[k], dst_ref=qbuf.at[k, me],
            send_sem=q_s.at[k, r], recv_sem=q_r.at[k, r],
            device_id={"blk": lax.rem(me + r, nb)}, device_id_type=MESH,
        )

    def q_arrival(k, r):
        return pltpu.make_async_remote_copy(
            src_ref=q_ref.at[k], dst_ref=qbuf.at[k, lax.rem(me + nb - r, nb)],
            send_sem=q_s.at[k, r], recv_sem=q_r.at[k, r],
            device_id={"blk": lax.rem(me + r, nb)}, device_id_type=MESH,
        )

    def p_copy(k, r):
        dst = lax.rem(me + r, nb)
        return pltpu.make_async_remote_copy(
            src_ref=psend.at[k, dst], dst_ref=prec.at[k, me],
            send_sem=p_s.at[k, r], recv_sem=p_r.at[k, r],
            device_id={"blk": dst}, device_id_type=MESH,
        )

    def p_arrival(k, r):
        return pltpu.make_async_remote_copy(
            src_ref=psend.at[k, lax.rem(me + r, nb)],
            dst_ref=prec.at[k, lax.rem(me + nb - r, nb)],
            send_sem=p_s.at[k, r], recv_sem=p_r.at[k, r],
            device_id={"blk": lax.rem(me + r, nb)}, device_id_type=MESH,
        )

    def each_peer(action):
        def step(r, carry):
            action(r)
            return carry
        lax.fori_loop(1, nb, step, 0)

    def send_queries(k, carry):
        each_peer(lambda r: q_copy(k, r).start())
        return carry

    lax.fori_loop(0, kv, send_queries, 0)

    loads[0].wait()
    loads[1].wait()
    owner = lax.broadcasted_iota(jnp.int32, (rows, slots), 0) // groups
    live = lax.broadcasted_iota(jnp.int32, (rows, slots), 1) < len_ref[:, :1]

    def own_head(k, carry):
        q = q_ref[k]
        s = jnp.zeros((rows, slots), F32)
        for i in range(n):
            part = lax.dot_general(q, sk[i, :, head_lanes(k)], NT, preferred_element_type=F32)
            s = jnp.where(owner == i, part, s)
        s = jnp.where(live, s * SCALE, -jnp.inf)
        own = jnp.sum(q.astype(F32) * nk_ref[k].astype(F32), axis=1, keepdims=True) * SCALE
        top = jnp.maximum(jnp.max(s, axis=1, keepdims=True), own)
        wf = jnp.exp(s - top).astype(BF16).astype(F32)
        own_w = jnp.exp(own - top).astype(BF16).astype(F32)
        acc = own_w * nv_ref[k].astype(F32)
        for i in range(n):
            part = jnp.where(owner == i, wf, 0.0).astype(BF16)
            acc += jnp.dot(part, sv[i, :, head_lanes(k)], preferred_element_type=F32)
        lacc[k] = acc
        lm[k] = jnp.broadcast_to(top, (rows, HD))
        lmass[k] = jnp.broadcast_to(jnp.sum(wf, axis=1, keepdims=True) + own_w, (rows, HD))
        return carry

    lax.fori_loop(0, kv, own_head, 0)

    loads[2].wait()
    loads[3].wait()
    stat[...] = jnp.zeros_like(stat)
    chunks = prefix // KEY_CHUNK
    lane = lax.broadcasted_iota(jnp.int32, (nb * rows, HD), 1)

    def prefix_head(k, carry):
        each_peer(lambda r: q_arrival(k, r).wait_recv())
        q = qbuf[k].reshape(nb * rows, HD)
        fold = None
        for c in range(chunks):
            s = lax.dot_general(
                q, pk[pl.ds(c * KEY_CHUNK, KEY_CHUNK), head_lanes(k)], NT,
                preferred_element_type=F32,
            )
            sbuf[:, pl.ds(c * KEY_CHUNK, KEY_CHUNK)] = s
            for p in range(KEY_CHUNK // HD):
                piece = s[:, p * HD:(p + 1) * HD]
                fold = piece if fold is None else jnp.maximum(fold, piece)
        top = (jnp.max(fold, axis=1, keepdims=True) * SCALE).astype(BF16).astype(F32)
        acc = jnp.zeros((nb * rows, HD), F32)
        total = jnp.zeros((nb * rows, HD), F32)
        for c in range(chunks):
            s = sbuf[:, pl.ds(c * KEY_CHUNK, KEY_CHUNK)]
            wb = jnp.exp(s * SCALE - top).astype(BF16)
            acc += jnp.dot(
                wb, pv[pl.ds(c * KEY_CHUNK, KEY_CHUNK), head_lanes(k)],
                preferred_element_type=F32,
            )
            wf = wb.astype(F32)
            for p in range(KEY_CHUNK // HD):
                total += wf[:, p * HD:(p + 1) * HD]
        mass = jnp.sum(total, axis=1, keepdims=True)
        high = mass.astype(BF16).astype(F32)
        psend[k] = acc.astype(BF16).reshape(nb, rows, HD)
        stat[...] = jnp.where(
            lane == k, top,
            jnp.where(lane == kv + k, high, jnp.where(lane == 2 * kv + k, mass - high, stat[...])),
        )
        each_peer(lambda r: p_copy(k, r).start())
        return carry

    lax.fori_loop(0, kv, prefix_head, 0)
    psend[kv] = stat[...].astype(BF16).reshape(nb, rows, HD)
    each_peer(lambda r: p_copy(kv, r).start())
    prec[:, me] = psend[:, me]

    def finish_copies(k, carry):
        each_peer(lambda r: p_arrival(k, r).wait_recv())
        return carry

    lax.fori_loop(0, kv + 1, finish_copies, 0)

    stats = [prec[kv, j].astype(F32) for j in range(nb)]
    for k in range(kv):
        top = lm[k]
        tops = [jnp.broadcast_to(st[:, k:k + 1], (rows, HD)) for st in stats]
        for t in tops:
            top = jnp.maximum(top, t)
        scale = jnp.exp(lm[k] - top)
        acc = lacc[k] * scale
        mass = lmass[k] * scale
        for j in range(nb):
            st = stats[j]
            scale = jnp.exp(tops[j] - top)
            block_mass = st[:, kv + k:kv + k + 1] + st[:, 2 * kv + k:2 * kv + k + 1]
            acc += prec[k, j].astype(F32) * scale
            mass += block_mass * scale
        abuf[mb, k] = (acc / mass).astype(BF16)

    def a_copy(r, slot):
        return pltpu.make_async_remote_copy(
            src_ref=abuf.at[mb], dst_ref=abuf.at[slot],
            send_sem=a_s.at[r], recv_sem=a_r.at[r],
            device_id={"batch": lax.rem(mb + r, nbt)}, device_id_type=MESH,
        )

    for r in range(1, nbt):
        a_copy(r, mb).start()
    for r in range(1, nbt):
        a_copy(r, lax.rem(mb + nbt - r, nbt)).wait_recv()

    for b in range(nbt):
        for k in range(kv):
            a32[b, k] = abuf[b, k].astype(F32)
            for g in range(groups):
                x[b * n:(b + 1) * n, (k * groups + g) * HD:(k * groups + g + 1) * HD] = a32[
                    b, k, pl.ds(g, n, stride=groups), :
                ]
    loads[4].wait()
    xb = x[...].astype(BF16)
    part_rows = osend.shape[1]

    def project(c, carry):
        cols = pl.ds(pl.multiple_of(c * COL_CHUNK, COL_CHUNK), COL_CHUNK)
        part = jnp.dot(xb, w[:, cols], preferred_element_type=F32)
        for t in range(nt):
            osend[t, :, cols] = part[t * part_rows:(t + 1) * part_rows]
        return carry

    lax.fori_loop(0, w.shape[1] // COL_CHUNK, project, 0)

    def o_copy(r, slot):
        dst = lax.rem(mt + r, nt)
        return pltpu.make_async_remote_copy(
            src_ref=osend.at[dst], dst_ref=orecv.at[slot],
            send_sem=o_s.at[r], recv_sem=o_r.at[r],
            device_id={"tensor": dst}, device_id_type=MESH,
        )

    for r in range(1, nt):
        o_copy(r, mt).start()
    result = osend[mt]
    for r in range(1, nt):
        slot = lax.rem(mt + nt - r, nt)
        o_copy(r, slot).wait_recv()
        result = result + orecv[slot]
    o_ref[...] = result.astype(o_ref.dtype)

    def finish_queries(k, carry):
        each_peer(lambda r: q_copy(k, r).wait_send())
        return carry

    def finish_sums(k, carry):
        each_peer(lambda r: p_copy(k, r).wait_send())
        return carry

    lax.fori_loop(0, kv, finish_queries, 0)
    lax.fori_loop(0, kv + 1, finish_sums, 0)
    for r in range(1, nbt):
        a_copy(r, mb).wait_send()
    for r in range(1, nt):
        o_copy(r, mt).wait_send()


def body(
    nb, nbt, nt,
    queries, new_keys, new_values, suffix_keys, suffix_values, suffix_lengths,
    prefix_keys, prefix_values, out_weight,
):
    n = queries.shape[0]
    kv = new_keys.shape[-1] // HD
    groups = queries.shape[-1] // new_keys.shape[-1]
    rows = n * groups
    slots = suffix_keys.shape[1]
    cols = out_weight.shape[1]
    prefix = prefix_keys.shape[0]
    part_rows = nbt * n // nt
    q = queries.reshape(n, kv, groups, HD).transpose(1, 0, 2, 3).reshape(kv, rows, HD)

    def spread(a):
        wide = jnp.broadcast_to(a.reshape(n, kv, HD).transpose(1, 0, 2)[:, :, None], (kv, n, groups, HD))
        return wide.reshape(kv, rows, HD)

    lengths = jnp.broadcast_to(suffix_lengths[:, None, None], (n, groups, HD)).reshape(rows, HD)
    vmem = pl.BlockSpec(memory_space=pltpu.VMEM)
    hbm = pl.BlockSpec(memory_space=pl.ANY)
    dma = pltpu.SemaphoreType.DMA
    flops = 4 * nb * rows * prefix * HD * kv + 2 * nbt * n * out_weight.size
    return pl.pallas_call(
        functools.partial(kernel, nb, nbt, nt, n),
        out_shape=jax.ShapeDtypeStruct((part_rows, cols), BF16),
        in_specs=[vmem] * 4 + [hbm] * 5,
        out_specs=vmem,
        scratch_shapes=[
            pltpu.VMEM(suffix_keys.shape, BF16),
            pltpu.VMEM(suffix_values.shape, BF16),
            pltpu.VMEM(prefix_keys.shape, BF16),
            pltpu.VMEM(prefix_values.shape, BF16),
            pltpu.VMEM(out_weight.shape, BF16),
            pltpu.VMEM((kv, nb, rows, HD), BF16),
            pltpu.VMEM((nb * rows, prefix), F32),
            pltpu.VMEM((nb * rows, HD), F32),
            pltpu.VMEM((kv + 1, nb, rows, HD), BF16),
            pltpu.VMEM((kv + 1, nb, rows, HD), BF16),
            pltpu.VMEM((kv, rows, HD), F32),
            pltpu.VMEM((kv, rows, HD), F32),
            pltpu.VMEM((kv, rows, HD), F32),
            pltpu.VMEM((nbt, kv, rows, HD), BF16),
            pltpu.VMEM((nbt, kv, rows, HD), F32),
            pltpu.VMEM((nbt * n, out_weight.shape[0]), F32),
            pltpu.VMEM((nt, part_rows, cols), F32),
            pltpu.VMEM((nt, part_rows, cols), F32),
            dma((5,)),
            dma((kv, nb)), dma((kv, nb)),
            dma((kv + 1, nb)), dma((kv + 1, nb)),
            dma((nbt,)), dma((nbt,)),
            dma((nt,)), dma((nt,)),
        ],
        compiler_params=pltpu.CompilerParams(
            collective_id=0, has_side_effects=True, vmem_limit_bytes=56 * 2**20
        ),
        cost_estimate=pl.CostEstimate(
            flops=flops,
            bytes_accessed=2 * (2 * suffix_keys.size + 2 * prefix_keys.size + out_weight.size),
            transcendentals=kv * rows * (nb * prefix + slots),
        ),
    )(q, spread(new_keys), spread(new_values), lengths, suffix_keys, suffix_values,
      prefix_keys, prefix_values, out_weight)


def solution(mesh):
    in_specs = (
        P(("blk", "batch"), "tensor"),
        P(("blk", "batch"), "tensor"),
        P(("blk", "batch"), "tensor"),
        P(("blk", "batch"), None, "tensor"),
        P(("blk", "batch"), None, "tensor"),
        P(("blk", "batch")),
        P("blk", "tensor"),
        P("blk", "tensor"),
        P("tensor", "batch"),
    )
    out_specs = P(("blk", "tensor"), "batch")
    sizes = (mesh.shape["blk"], mesh.shape["batch"], mesh.shape["tensor"])
    return jax.shard_map(
        functools.partial(body, *sizes), mesh=mesh, in_specs=in_specs, out_specs=out_specs,
        check_vma=False,
    )
```

time: 167 us -> 39.6 us (0.24)
  blocking collectives: 84.5 us -> 0 us
  Pallas kernels: 0 us -> 33 us
  waiting for transfers between devices: 25.5 us -> 0 us
  matrix products: 21.2 us -> 0 us
  between operations: 14.8 us -> 0.01 us
  local copies, waits for them, and re-layouts: 13.7 us -> 6.22 us
  other arithmetic: 6.6 us -> 0 us
    unnamed x2 -> x0, blocking collectives: 34.8 us -> none
    pallas_call x0 -> x1, Pallas kernels: none -> 33 us  [body(): pl.pallas_call(functools.partial(kernel, nb, nbt, nt, n), out_shape=jax.S...]
    pmax x1 -> x0, blocking collectives: 29.2 us -> none  [body(): full_top = lax.pmax(joined_top, 'blk')]
    unnamed x2 -> x0, waiting for transfers between devices: 25.5 us -> none
    dot_general x6 -> x0, matrix products: 21.2 us -> none  [the longest x1 8.04 us: body(): jnp.dot(lax.all_gather(attended, 'batch', axis=0, tiled=True), out_weight...]
    all_gather x2 -> x0, blocking collectives: 20.5 us -> none  [the longest x1 15.9 us: body(): gathered = lax.all_gather(queries, 'blk', axis=0, tiled=True)]
    reshape x9 -> x4, local copies, waits for them, and re-layouts: 8.88 us -> 3.4 us  [the longest x2 1.39 us: spread(): a.reshape(n, kv, HD).transpose(1, 0, 2)[:, :, None]]
    convert_element_type x4 -> x0, other arithmetic: 4.29 us -> none  [the longest x1 4.16 us: group_sums(): jnp.exp(scores - row_top.reshape(row_count, kv_count, -1)[..., None])]
  transfers between devices with their start and end apart: 1 -> 0, of which waited for: 1 -> 0; matrix products, arithmetic and copies ran while one was open for 1% -> 0% of each run, Pallas kernels for 0% -> 0%
where the time goes in v1:
time: 39.6 us; the launch traced here: 39.3 us
  Pallas kernels  33 us (83%)
  local copies, waits for them, and re-layouts  6.22 us (16%)
    pallas_call x1, Pallas kernels, body(): pl.pallas_call(functools.partial(kernel, nb, nbt, nt, n), out_shape=jax.S...  33 us
    broadcast_in_dim x3, local copies, waits for them, and re-layouts, body(): jnp.broadcast_to(suffix_lengths[:, None, None], (n, groups, HD))  1.48 us
    reshape x2, local copies, waits for them, and re-layouts, spread(): a.reshape(n, kv, HD).transpose(1, 0, 2)[:, :, None]  1.39 us
    reshape x1, local copies, waits for them, and re-layouts, body(): queries.reshape(n, kv, groups, HD).transpose(1, 0, 2, 3)  1.38 us
    unnamed x1, local copies, waits for them, and re-layouts  1.33 us

profile of v1, /device:TPU:0, one launch (start us, length us, event | category | flops | bytes accessed | tf_op | source)
XLA Modules:
  0.0 39.3 jit_solution(9695498258995403466)
XLA Ops:
  0.0 0.7 %broadcast_in_dim.24 = s32[4,8]{1,0:T(4,128)S(1)} broadcast(s32[4]{0:T(128)} %param.14), dimensions={0} | broadcast | bytes 144 | tf_op jit(solution)/shard_map/broadcast_in_dim | solution.py:281
  0.7 0.1 broadcast_in_dim.25
  0.8 0.7 %reshape.25 = bf16[4,4,128]{2,1,0:T(4,128)(2,1)S(1)} reshape(bf16[4,512]{1,0:T(4,128)(2,1)} %param.10) | data formatting | bytes 8192 | tf_op jit(solution)/shard_map/reshape | solution.py:278
  1.5 0.7 %reshape.27 = bf16[4,4,128]{2,1,0:T(4,128)(2,1)S(1)} reshape(bf16[4,512]{1,0:T(4,128)(2,1)} %param.11) | data formatting | bytes 8192 | tf_op jit(solution)/shard_map/reshape | solution.py:278
  2.2 0.7 %broadcast_in_dim.26.len_ref = s32[32,128]{1,0:T(8,128)} broadcast(s32[32]{0:T(128)S(1)} %broadcast_in_dim.25), dimensions={0} | broadcast | bytes 16512 | tf_op jit(solution)/shard_map/broadcast_in_dim | solution.py:281
  2.9 1.4 %copy_bitcast_fusion.1.q_ref = bf16[4,32,128]{2,1,0:T(8,128)(2,1)} fusion(bf16[1,4,32,128]{3,1,2,0:T(4,128)(2,1)} %bitcast.15), kind=kLoop, calls=%fused_computation.1 | loop fusion | bytes 65536 | tf_op jit(solution)/shard_map/reshape | solution.py:275
  4.3 0.6 %broadcast_bitcast_fusion = (bf16[4,32,128]{2,1,0:T(8,128)(2,1)}, bf16[4,32,128]{2,1,0:T(8,128)(2,1)}) fusion(bf16[4,4,128]{2,1,0:T(4,128)(2,1)S(1)} %copy.12, bf16[4,4,128]{2,1,0:T(4,128)(2,1)S(1)} %copy.11), kind=kLoop, calls=%fused_computation.2 | loop fusion | bytes 73728 | tf_op jit(solution)/shard_map/reshape | solution.py:279
  4.9 33.0 %shard_map.91 = bf16[4,2048]{1,0:T(4,128)(2,1)} custom-call(bf16[4,32,128]{2,1,0:T(8,128)(2,1)} %copy_bitcast_fusion.1.q_ref, bf16[4,32,128]{2,1,0:T(8,128)(2,1)} %get-tuple-element.6.nk_ref, bf16[4,32,128]{2,1,0:T(8,128)(2,1)} %get-tuple-element.5.nv_ref, s32[32,128]{1,0:T(8,128)} %broadcast_in_dim.26.len_ref, bf16[4,512,512]{2,1,0:T(8,128)(2,1)} %sk_hbm.1, ...), custom_call_target="tpu_custom_call" | custom-call | flops 1207959552 | bytes 25165824 | tf_op jit(solution)/shard_map/pallas_call | solution.py:286
  37.9 1.3 %copy.18 = bf16[4,2048]{1,0:T(4,128)(2,1)} copy(bf16[4,2048]{1,0:T(4,128)(2,1)} %shard_map.91) | data formatting | bytes 32768
  (2 shorter events, 0.0 us)

commit v2 on v1

v2 whole, which is shorter than its diff:
```python
import functools

import jax
import jax.numpy as jnp
from jax import lax
from jax.experimental import pallas as pl
from jax.experimental.pallas import tpu as pltpu
from jax.sharding import PartitionSpec as P

HD = 128
SCALE = HD ** (-0.5)
F32 = jnp.float32
BF16 = jnp.bfloat16
MESH = pl.DeviceIdType.MESH
NT = (((1,), (1,)), ((), ()))
KEY_CHUNK = 512
COL_CHUNK = 256


def head_lanes(k):
    return pl.ds(pl.multiple_of(k * HD, HD), HD)


def kernel(
    nb, nbt, nt, n,
    q_ref, nk_ref, nv_ref, len_ref, sk_hbm, sv_hbm, pk_hbm, pv_hbm, w_hbm,
    o_ref,
    sk, sv, pk, pv, w, q32, nk32, nv32, qsrc, qbuf, sbuf, stat, psend, prec, lacc, lm, lmass,
    abuf, a32, x, osend, orecv,
    lsem, k_s, k_r, q_s, q_r, p_s, p_r, a_s, a_r, o_s, o_r,
):
    kv, rows, _ = q32.shape
    groups = rows // n
    half = kv // 2
    slots = sk.shape[1]
    prefix = pk.shape[1]
    me = lax.axis_index("blk")
    mb = lax.axis_index("batch")
    mt = lax.axis_index("tensor")
    core = lax.rem(me, 2)
    pair = me + 1 - 2 * core

    def half_lanes(c):
        return pl.ds(pl.multiple_of(c * half * HD, half * HD), half * HD)

    barrier = pltpu.get_barrier_semaphore()
    for axis, mine, size in (("blk", me, nb), ("batch", mb, nbt), ("tensor", mt, nt)):
        for r in range(1, size):
            pl.semaphore_signal(
                barrier, inc=1, device_id={axis: lax.rem(mine + r, size)}, device_id_type=MESH
            )
    loads = [
        pltpu.make_async_copy(src, dst, lsem.at[i])
        for i, (src, dst) in enumerate([
            (sk_hbm, sk), (sv_hbm, sv), (pk_hbm.at[:, half_lanes(core)], pk.at[0]),
            (pv_hbm.at[:, half_lanes(core)], pv.at[0]), (w_hbm, w),
        ])
    ]
    for load in loads[:4]:
        load.start()

    qf = q_ref[...].astype(F32)
    for k in range(kv):
        for g in range(groups):
            h = k * groups + g
            q32[k, pl.ds(g, n, stride=groups), :] = qf[:, h * HD:(h + 1) * HD]
        qsrc[k] = q32[k].astype(BF16)
    qbuf[me] = qsrc[pl.ds(core * half, half)]
    pl.semaphore_wait(barrier, nb + nbt + nt - 3)

    def q_copy(r, slot):
        dst = lax.rem(me + r, nb)
        return pltpu.make_async_remote_copy(
            src_ref=qsrc.at[pl.ds(lax.rem(dst, 2) * half, half)], dst_ref=qbuf.at[slot],
            send_sem=q_s.at[r], recv_sem=q_r.at[r],
            device_id={"blk": dst}, device_id_type=MESH,
        )

    def pair_copy(i, src, dst):
        return pltpu.make_async_remote_copy(
            src_ref=src.at[:, half_lanes(1 - core)], dst_ref=dst.at[1],
            send_sem=k_s.at[i], recv_sem=k_r.at[i],
            device_id={"blk": pair}, device_id_type=MESH,
        )

    def p_copy(part, r, slot):
        dst = lax.rem(me + r, nb)
        span = pl.ds(0, half - 1) if part == 0 else pl.ds(half - 1, 2)
        return pltpu.make_async_remote_copy(
            src_ref=psend.at[dst, span], dst_ref=prec.at[slot, span],
            send_sem=p_s.at[part, r], recv_sem=p_r.at[part, r],
            device_id={"blk": dst}, device_id_type=MESH,
        )

    def source(r):
        return lax.rem(me + nb - r, nb)

    def each_peer(action):
        def step(r, carry):
            action(r)
            return carry
        lax.fori_loop(1, nb, step, 0)

    each_peer(lambda r: q_copy(r, me).start())
    swaps = [pair_copy(0, pk_hbm, pk), pair_copy(1, pv_hbm, pv)]
    for swap in swaps:
        swap.start()
    loads[4].start()

    nkf, nvf = nk_ref[...].astype(F32), nv_ref[...].astype(F32)
    for k in range(kv):
        for i in range(n):
            span = slice(i * groups, (i + 1) * groups)
            nk32[k, span, :] = jnp.broadcast_to(nkf[i:i + 1, k * HD:(k + 1) * HD], (groups, HD))
            nv32[k, span, :] = jnp.broadcast_to(nvf[i:i + 1, k * HD:(k + 1) * HD], (groups, HD))

    loads[0].wait()
    loads[1].wait()
    owner = lax.broadcasted_iota(jnp.int32, (rows, slots), 0) // groups
    lengths = jnp.zeros((rows, slots), jnp.int32)
    for i in range(n):
        lengths = jnp.where(owner == i, len_ref[i], lengths)
    live = lax.broadcasted_iota(jnp.int32, (rows, slots), 1) < lengths

    def own_head(k, carry):
        q = qsrc[k]
        s = jnp.zeros((rows, slots), F32)
        for i in range(n):
            part = lax.dot_general(q, sk[i, :, head_lanes(k)], NT, preferred_element_type=F32)
            s = jnp.where(owner == i, part, s)
        s = jnp.where(live, s * SCALE, -jnp.inf)
        own = jnp.sum(q32[k] * nk32[k], axis=1, keepdims=True) * SCALE
        top = jnp.maximum(jnp.max(s, axis=1, keepdims=True), own)
        wf = jnp.exp(s - top).astype(BF16).astype(F32)
        own_w = jnp.exp(own - top).astype(BF16).astype(F32)
        acc = own_w * nv32[k]
        for i in range(n):
            part = jnp.where(owner == i, wf, 0.0).astype(BF16)
            acc += jnp.dot(part, sv[i, :, head_lanes(k)], preferred_element_type=F32)
        lacc[k] = acc
        lm[k] = jnp.broadcast_to(top, (rows, HD))
        lmass[k] = jnp.broadcast_to(jnp.sum(wf, axis=1, keepdims=True) + own_w, (rows, HD))
        return carry

    lax.fori_loop(0, kv, own_head, 0)

    loads[2].wait()
    loads[3].wait()
    for swap in swaps:
        swap.wait_recv()
    each_peer(lambda r: q_copy(r, source(r)).wait_recv())
    chunks = [
        (b, pl.ds(c * KEY_CHUNK, KEY_CHUNK), pl.ds(b * prefix + c * KEY_CHUNK, KEY_CHUNK))
        for b in range(2) for c in range(prefix // KEY_CHUNK)
    ]
    lane = lax.broadcasted_iota(jnp.int32, (nb * rows, HD), 1)
    stat[...] = jnp.zeros_like(stat)

    def prefix_head(k):
        lanes = pl.ds(k * HD, HD)
        q = qbuf[:, k].reshape(nb * rows, HD)
        fold = None
        for b, span, place in chunks:
            s = lax.dot_general(q, pk[b, span, lanes], NT, preferred_element_type=F32)
            sbuf[:, place] = s
            for p in range(KEY_CHUNK // HD):
                piece = s[:, p * HD:(p + 1) * HD]
                fold = piece if fold is None else jnp.maximum(fold, piece)
        top = (jnp.max(fold, axis=1, keepdims=True) * SCALE).astype(BF16).astype(F32)
        acc = jnp.zeros((nb * rows, HD), F32)
        total = jnp.zeros((nb * rows, HD), F32)
        for b, span, place in chunks:
            wb = jnp.exp(sbuf[:, place] * SCALE - top).astype(BF16)
            acc += jnp.dot(wb, pv[b, span, lanes], preferred_element_type=F32)
            wf = wb.astype(F32)
            for p in range(KEY_CHUNK // HD):
                total += wf[:, p * HD:(p + 1) * HD]
        mass = jnp.sum(total, axis=1, keepdims=True)
        high = mass.astype(BF16).astype(F32)
        psend[:, k] = acc.astype(BF16).reshape(nb, rows, HD)
        stat[...] = jnp.where(
            lane == k, top,
            jnp.where(
                lane == half + k, high, jnp.where(lane == 2 * half + k, mass - high, stat[...])
            ),
        )

    for k in range(half):
        prefix_head(k)
        if k == half - 2:
            each_peer(lambda r: p_copy(0, r, me).start())
    psend[:, half] = stat[...].astype(BF16).reshape(nb, rows, HD)
    each_peer(lambda r: p_copy(1, r, me).start())
    prec[me] = psend[me]
    each_peer(lambda r: p_copy(0, r, source(r)).wait_recv())
    each_peer(lambda r: p_copy(1, r, source(r)).wait_recv())

    stats = [prec[j, half].astype(F32) for j in range(nb)]
    for h in range(kv):
        k = h % half
        sources = range(h // half, nb, 2)
        top = lm[h]
        tops = {j: jnp.broadcast_to(stats[j][:, k:k + 1], (rows, HD)) for j in sources}
        for j in sources:
            top = jnp.maximum(top, tops[j])
        scale = jnp.exp(lm[h] - top)
        acc = lacc[h] * scale
        mass = lmass[h] * scale
        for j in sources:
            st = stats[j]
            scale = jnp.exp(tops[j] - top)
            acc += prec[j, k].astype(F32) * scale
            mass += scale * (
                st[:, half + k:half + k + 1] + st[:, 2 * half + k:2 * half + k + 1]
            )
        abuf[mb, h] = (acc / mass).astype(BF16)

    def a_copy(r, slot):
        return pltpu.make_async_remote_copy(
            src_ref=abuf.at[mb], dst_ref=abuf.at[slot],
            send_sem=a_s.at[r], recv_sem=a_r.at[r],
            device_id={"batch": lax.rem(mb + r, nbt)}, device_id_type=MESH,
        )

    for r in range(1, nbt):
        a_copy(r, mb).start()
    for r in range(1, nbt):
        a_copy(r, lax.rem(mb + nbt - r, nbt)).wait_recv()

    for b in range(nbt):
        for k in range(kv):
            a32[b, k] = abuf[b, k].astype(F32)
            for g in range(groups):
                x[b * n:(b + 1) * n, (k * groups + g) * HD:(k * groups + g + 1) * HD] = a32[
                    b, k, pl.ds(g, n, stride=groups), :
                ]
    loads[4].wait()
    xb = x[...].astype(BF16)
    part_rows = osend.shape[1]

    def project(c, carry):
        cols = pl.ds(pl.multiple_of(c * COL_CHUNK, COL_CHUNK), COL_CHUNK)
        part = jnp.dot(xb, w[:, cols], preferred_element_type=F32)
        for t in range(nt):
            osend[t, :, cols] = part[t * part_rows:(t + 1) * part_rows]
        return carry

    lax.fori_loop(0, w.shape[1] // COL_CHUNK, project, 0)

    def o_copy(r, slot):
        dst = lax.rem(mt + r, nt)
        return pltpu.make_async_remote_copy(
            src_ref=osend.at[dst], dst_ref=orecv.at[slot],
            send_sem=o_s.at[r], recv_sem=o_r.at[r],
            device_id={"tensor": dst}, device_id_type=MESH,
        )

    for r in range(1, nt):
        o_copy(r, mt).start()
    result = osend[mt]
    for r in range(1, nt):
        slot = lax.rem(mt + nt - r, nt)
        o_copy(r, slot).wait_recv()
        result = result + orecv[slot]
    o_ref[...] = result

    each_peer(lambda r: q_copy(r, me).wait_send())
    each_peer(lambda r: p_copy(0, r, me).wait_send())
    each_peer(lambda r: p_copy(1, r, me).wait_send())
    for swap in swaps:
        swap.wait_send()
    for r in range(1, nbt):
        a_copy(r, mb).wait_send()
    for r in range(1, nt):
        o_copy(r, mt).wait_send()


def body(
    nb, nbt, nt,
    queries, new_keys, new_values, suffix_keys, suffix_values, suffix_lengths,
    prefix_keys, prefix_values, out_weight,
):
    n = queries.shape[0]
    kv = new_keys.shape[-1] // HD
    groups = queries.shape[-1] // new_keys.shape[-1]
    rows = n * groups
    slots = suffix_keys.shape[1]
    cols = out_weight.shape[1]
    prefix = prefix_keys.shape[0]
    part_rows = nbt * n // nt
    half = kv // 2
    vmem = pl.BlockSpec(memory_space=pltpu.VMEM)
    smem = pl.BlockSpec(memory_space=pltpu.SMEM)
    hbm = pl.BlockSpec(memory_space=pl.ANY)
    dma = pltpu.SemaphoreType.DMA
    flops = 4 * nb * rows * prefix * HD * kv + 2 * nbt * n * out_weight.size
    return pl.pallas_call(
        functools.partial(kernel, nb, nbt, nt, n),
        out_shape=jax.ShapeDtypeStruct((part_rows, cols), F32),
        in_specs=[vmem] * 3 + [smem] + [hbm] * 5,
        out_specs=vmem,
        scratch_shapes=[
            pltpu.VMEM(suffix_keys.shape, BF16),
            pltpu.VMEM(suffix_values.shape, BF16),
            pltpu.VMEM((2, prefix, half * HD), BF16),
            pltpu.VMEM((2, prefix, half * HD), BF16),
            pltpu.VMEM(out_weight.shape, BF16),
            pltpu.VMEM((kv, rows, HD), F32),
            pltpu.VMEM((kv, rows, HD), F32),
            pltpu.VMEM((kv, rows, HD), F32),
            pltpu.VMEM((kv, rows, HD), BF16),
            pltpu.VMEM((nb, half, rows, HD), BF16),
            pltpu.VMEM((nb * rows, 2 * prefix), F32),
            pltpu.VMEM((nb * rows, HD), F32),
            pltpu.VMEM((nb, half + 1, rows, HD), BF16),
            pltpu.VMEM((nb, half + 1, rows, HD), BF16),
            pltpu.VMEM((kv, rows, HD), F32),
            pltpu.VMEM((kv, rows, HD), F32),
            pltpu.VMEM((kv, rows, HD), F32),
            pltpu.VMEM((nbt, kv, rows, HD), BF16),
            pltpu.VMEM((nbt, kv, rows, HD), F32),
            pltpu.VMEM((nbt * n, out_weight.shape[0]), F32),
            pltpu.VMEM((nt, part_rows, cols), F32),
            pltpu.VMEM((nt, part_rows, cols), F32),
            dma((5,)),
            dma((2,)), dma((2,)),
            dma((nb,)), dma((nb,)),
            dma((2, nb)), dma((2, nb)),
            dma((nbt,)), dma((nbt,)),
            dma((nt,)), dma((nt,)),
        ],
        compiler_params=pltpu.CompilerParams(
            collective_id=0, has_side_effects=True, vmem_limit_bytes=56 * 2**20
        ),
        cost_estimate=pl.CostEstimate(
            flops=flops,
            bytes_accessed=2 * (2 * suffix_keys.size + 2 * prefix_keys.size + out_weight.size),
            transcendentals=kv * rows * (nb * prefix + slots),
        ),
    )(queries, new_keys, new_values, suffix_lengths, suffix_keys, suffix_values,
      prefix_keys, prefix_values, out_weight).astype(BF16)


def solution(mesh):
    in_specs = (
        P(("blk", "batch"), "tensor"),
        P(("blk", "batch"), "tensor"),
        P(("blk", "batch"), "tensor"),
        P(("blk", "batch"), None, "tensor"),
        P(("blk", "batch"), None, "tensor"),
        P(("blk", "batch")),
        P("blk", "tensor"),
        P("blk", "tensor"),
        P("tensor", "batch"),
    )
    out_specs = P(("blk", "tensor"), "batch")
    sizes = (mesh.shape["blk"], mesh.shape["batch"], mesh.shape["tensor"])
    return jax.shard_map(
        functools.partial(body, *sizes), mesh=mesh, in_specs=in_specs, out_specs=out_specs,
        check_vma=False,
    )
```

time: 39.6 us -> 32.5 us (0.82)
  local copies, waits for them, and re-layouts: 6.22 us -> 0 us
  Pallas kernels: 33 us -> 30.9 us
  other arithmetic: 0 us -> 1.37 us
    reshape x4 -> x0, local copies, waits for them, and re-layouts: 3.4 us -> none  [the longest x2 1.39 us: spread(): a.reshape(n, kv, HD).transpose(1, 0, 2)[:, :, None]]
    pallas_call x1, Pallas kernels: 33 us -> 30.9 us  [body(): pl.pallas_call(functools.partial(kernel, nb, nbt, nt, n), out_shape=jax.S...]
    broadcast_in_dim x3 -> x0, local copies, waits for them, and re-layouts: 1.48 us -> none  [body(): jnp.broadcast_to(suffix_lengths[:, None, None], (n, groups, HD))]
    convert_element_type x0 -> x1, other arithmetic: none -> 1.37 us  [body(): return pl.pallas_call(functools.partial(kernel, nb, nbt, nt, n), out_shap...]
    unnamed x1 -> x0, local copies, waits for them, and re-layouts: 1.33 us -> none
where the time goes in v2:
time: 32.5 us; the launch traced here: 32.3 us
  Pallas kernels  30.9 us (95%)
  other arithmetic  1.37 us (4%)
    pallas_call x1, Pallas kernels, body(): pl.pallas_call(functools.partial(kernel, nb, nbt, nt, n), out_shape=jax.S...  30.9 us
    convert_element_type x1, other arithmetic, body(): return pl.pallas_call(functools.partial(kernel, nb, nbt, nt, n), out_shap...  1.37 us

profile of v2, /device:TPU:0, one launch (start us, length us, event | category | flops | bytes accessed | tf_op | source)
XLA Modules:
  0.0 32.3 jit_solution(3301912803777821278)
XLA Ops:
  0.0 30.9 %shard_map.91 = f32[4,2048]{1,0:T(4,128)} custom-call(bf16[4,4096]{1,0:T(4,128)(2,1)} %q_ref.1, bf16[4,512]{1,0:T(4,128)(2,1)} %nk_ref.1, bf16[4,512]{1,0:T(4,128)(2,1)} %nv_ref.1, s32[4]{0:T(128)} %len_ref.1, bf16[4,512,512]{2,1,0:T(8,128)(2,1)} %sk_hbm.1, bf16[4,512,512]{2,1,0:T(8,128)(2,1)} %sv_hbm.1, bf16[2048,512]{1,0:T(8,128)(2,1)} %pk_hbm.1, ...), custom_call_target="tpu_custom_call" | custom-call | flops 1207959552 | bytes 25165824 | tf_op jit(solution)/shard_map/pallas_call | solution.py:297
  30.9 1.4 %convert_element_type.3 = bf16[4,2048]{1,0:T(4,128)(2,1)} convert(f32[4,2048]{1,0:T(4,128)} %shard_map.91) | non-fusion elementwise | flops 8192 | bytes 49152 | tf_op jit(solution)/shard_map/convert_element_type | solution.py:341

commit v3 on v2

--- a/solution.py
+++ b/solution.py
@@ -25,7 +25,7 @@
     nb, nbt, nt, n,
     q_ref, nk_ref, nv_ref, len_ref, sk_hbm, sv_hbm, pk_hbm, pv_hbm, w_hbm,
     o_ref,
-    sk, sv, pk, pv, w, q32, nk32, nv32, qsrc, qbuf, sbuf, stat, psend, prec, lacc, lm, lmass,
+    sk, sv, pk, pv, w, q32, nk32, nv32, qsrc, qbuf, sbuf, psend, prec, lacc, lm, lmass,
     abuf, a32, x, osend, orecv,
     lsem, k_s, k_r, q_s, q_r, p_s, p_r, a_s, a_r, o_s, o_r,
 ):
@@ -56,7 +56,7 @@
             (pv_hbm.at[:, half_lanes(core)], pv.at[0]), (w_hbm, w),
         ])
     ]
-    for load in loads[:4]:
+    for load in loads:
         load.start()
 
     qf = q_ref[...].astype(F32)
@@ -83,12 +83,11 @@
             device_id={"blk": pair}, device_id_type=MESH,
         )
 
-    def p_copy(part, r, slot):
+    def p_copy(k, r, slot):
         dst = lax.rem(me + r, nb)
-        span = pl.ds(0, half - 1) if part == 0 else pl.ds(half - 1, 2)
-        return pltpu.make_async_remote_copy(
-            src_ref=psend.at[dst, span], dst_ref=prec.at[slot, span],
-            send_sem=p_s.at[part, r], recv_sem=p_r.at[part, r],
+        return pltpu.make_async_remote_copy(
+            src_ref=psend.at[k, dst], dst_ref=prec.at[k, slot],
+            send_sem=p_s.at[k, r], recv_sem=p_r.at[k, r],
             device_id={"blk": dst}, device_id_type=MESH,
         )
 
@@ -105,7 +104,6 @@
     swaps = [pair_copy(0, pk_hbm, pk), pair_copy(1, pv_hbm, pv)]
     for swap in swaps:
         swap.start()
-    loads[4].start()
 
     nkf, nvf = nk_ref[...].astype(F32), nv_ref[...].astype(F32)
     for k in range(kv):
@@ -154,7 +152,6 @@
         for b in range(2) for c in range(prefix // KEY_CHUNK)
     ]
     lane = lax.broadcasted_iota(jnp.int32, (nb * rows, HD), 1)
-    stat[...] = jnp.zeros_like(stat)
 
     def prefix_head(k):
         lanes = pl.ds(k * HD, HD)
@@ -177,75 +174,76 @@
                 total += wf[:, p * HD:(p + 1) * HD]
         mass = jnp.sum(total, axis=1, keepdims=True)
         high = mass.astype(BF16).astype(F32)
-        psend[:, k] = acc.astype(BF16).reshape(nb, rows, HD)
-        stat[...] = jnp.where(
-            lane == k, top,
-            jnp.where(
-                lane == half + k, high, jnp.where(lane == 2 * half + k, mass - high, stat[...])
-            ),
-        )
+        stat = jnp.where(lane == 0, top, jnp.where(lane == 1, high, mass - high))
+        psend[k, :, 0] = acc.astype(BF16).reshape(nb, rows, HD)
+        psend[k, :, 1] = stat.astype(BF16).reshape(nb, rows, HD)
 
     for k in range(half):
         prefix_head(k)
-        if k == half - 2:
-            each_peer(lambda r: p_copy(0, r, me).start())
-    psend[:, half] = stat[...].astype(BF16).reshape(nb, rows, HD)
-    each_peer(lambda r: p_copy(1, r, me).start())
-    prec[me] = psend[me]
-    each_peer(lambda r: p_copy(0, r, source(r)).wait_recv())
-    each_peer(lambda r: p_copy(1, r, source(r)).wait_recv())
-
-    stats = [prec[j, half].astype(F32) for j in range(nb)]
-    for h in range(kv):
-        k = h % half
-        sources = range(h // half, nb, 2)
-        top = lm[h]
-        tops = {j: jnp.broadcast_to(stats[j][:, k:k + 1], (rows, HD)) for j in sources}
-        for j in sources:
-            top = jnp.maximum(top, tops[j])
-        scale = jnp.exp(lm[h] - top)
-        acc = lacc[h] * scale
-        mass = lmass[h] * scale
-        for j in sources:
-            st = stats[j]
-            scale = jnp.exp(tops[j] - top)
-            acc += prec[j, k].astype(F32) * scale
-            mass += scale * (
-                st[:, half + k:half + k + 1] + st[:, 2 * half + k:2 * half + k + 1]
-            )
-        abuf[mb, h] = (acc / mass).astype(BF16)
-
-    def a_copy(r, slot):
-        return pltpu.make_async_remote_copy(
-            src_ref=abuf.at[mb], dst_ref=abuf.at[slot],
-            send_sem=a_s.at[r], recv_sem=a_r.at[r],
+        each_peer(functools.partial(lambda k, r: p_copy(k, r, me).start(), k))
+        prec[k, me] = psend[k, me]
+
+    def join(k):
+        for p in range(2):
+            h = p * half + k
+            sources = range(p, nb, 2)
+            stats = {j: prec[k, j, 1].astype(F32) for j in sources}
+            tops = {j: jnp.broadcast_to(stats[j][:, :1], (rows, HD)) for j in sources}
+            top = lm[h]
+            for j in sources:
+                top = jnp.maximum(top, tops[j])
+            scale = jnp.exp(lm[h] - top)
+            acc = lacc[h] * scale
+            mass = lmass[h] * scale
+            for j in sources:
+                scale = jnp.exp(tops[j] - top)
+                acc += prec[k, j, 0].astype(F32) * scale
+                mass += scale * (stats[j][:, 1:2] + stats[j][:, 2:3])
+            abuf[k, mb, p] = (acc / mass).astype(BF16)
+
+    def a_copy(k, r, slot):
+        return pltpu.make_async_remote_copy(
+            src_ref=abuf.at[k, mb], dst_ref=abuf.at[k, slot],
+            send_sem=a_s.at[k, r], recv_sem=a_r.at[k, r],
             device_id={"batch": lax.rem(mb + r, nbt)}, device_id_type=MESH,
         )
 
-    for r in range(1, nbt):
-        a_copy(r, mb).start()
-    for r in range(1, nbt):
-        a_copy(r, lax.rem(mb + nbt - r, nbt)).wait_recv()
-
-    for b in range(nbt):
-        for k in range(kv):
-            a32[b, k] = abuf[b, k].astype(F32)
-            for g in range(groups):
-                x[b * n:(b + 1) * n, (k * groups + g) * HD:(k * groups + g + 1) * HD] = a32[
-                    b, k, pl.ds(g, n, stride=groups), :
-                ]
-    loads[4].wait()
-    xb = x[...].astype(BF16)
     part_rows = osend.shape[1]
-
-    def project(c, carry):
-        cols = pl.ds(pl.multiple_of(c * COL_CHUNK, COL_CHUNK), COL_CHUNK)
-        part = jnp.dot(xb, w[:, cols], preferred_element_type=F32)
-        for t in range(nt):
-            osend[t, :, cols] = part[t * part_rows:(t + 1) * part_rows]
-        return carry
-
-    lax.fori_loop(0, w.shape[1] // COL_CHUNK, project, 0)
+    depth = groups * HD
+
+    def project(k):
+        for b in range(nbt):
+            for p in range(2):
+                h = p * half + k
+                a32[b, h] = abuf[k, b, p].astype(F32)
+                for g in range(groups):
+                    x[b * n:(b + 1) * n, h * depth + g * HD:h * depth + (g + 1) * HD] = a32[
+                        b, h, pl.ds(g, n, stride=groups), :
+                    ]
+        spans = [pl.ds((p * half + k) * depth, depth) for p in range(2)]
+        xs = [x[:, span].astype(BF16) for span in spans]
+
+        def column_block(c, carry):
+            cols = pl.ds(pl.multiple_of(c * COL_CHUNK, COL_CHUNK), COL_CHUNK)
+            part = jnp.dot(xs[0], w[spans[0], cols], preferred_element_type=F32)
+            part += jnp.dot(xs[1], w[spans[1], cols], preferred_element_type=F32)
+            for t in range(nt):
+                piece = part[t * part_rows:(t + 1) * part_rows]
+                osend[t, :, cols] = piece if k == 0 else osend[t, :, cols] + piece
+            return carry
+
+        lax.fori_loop(0, w.shape[1] // COL_CHUNK, column_block, 0)
+
+    for k in range(half):
+        each_peer(functools.partial(lambda k, r: p_copy(k, r, source(r)).wait_recv(), k))
+        join(k)
+        for r in range(1, nbt):
+            a_copy(k, r, mb).start()
+        for r in range(1, nbt):
+            a_copy(k, r, lax.rem(mb + nbt - r, nbt)).wait_recv()
+        if k == 0:
+            loads[4].wait()
+        project(k)
 
     def o_copy(r, slot):
         dst = lax.rem(mt + r, nt)
@@ -265,12 +263,12 @@
     o_ref[...] = result
 
     each_peer(lambda r: q_copy(r, me).wait_send())
-    each_peer(lambda r: p_copy(0, r, me).wait_send())
-    each_peer(lambda r: p_copy(1, r, me).wait_send())
+    for k in range(half):
+        each_peer(functools.partial(lambda k, r: p_copy(k, r, me).wait_send(), k))
+        for r in range(1, nbt):
+            a_copy(k, r, mb).wait_send()
     for swap in swaps:
         swap.wait_send()
-    for r in range(1, nbt):
-        a_copy(r, mb).wait_send()
     for r in range(1, nt):
         o_copy(r, mt).wait_send()
 
@@ -311,13 +309,12 @@
             pltpu.VMEM((kv, rows, HD), BF16),
             pltpu.VMEM((nb, half, rows, HD), BF16),
             pltpu.VMEM((nb * rows, 2 * prefix), F32),
-            pltpu.VMEM((nb * rows, HD), F32),
-            pltpu.VMEM((nb, half + 1, rows, HD), BF16),
-            pltpu.VMEM((nb, half + 1, rows, HD), BF16),
-            pltpu.VMEM((kv, rows, HD), F32),
-            pltpu.VMEM((kv, rows, HD), F32),
-            pltpu.VMEM((kv, rows, HD), F32),
-            pltpu.VMEM((nbt, kv, rows, HD), BF16),
+            pltpu.VMEM((half, nb, 2, rows, HD), BF16),
+            pltpu.VMEM((half, nb, 2, rows, HD), BF16),
+            pltpu.VMEM((kv, rows, HD), F32),
+            pltpu.VMEM((kv, rows, HD), F32),
+            pltpu.VMEM((kv, rows, HD), F32),
+            pltpu.VMEM((half, nbt, 2, rows, HD), BF16),
             pltpu.VMEM((nbt, kv, rows, HD), F32),
             pltpu.VMEM((nbt * n, out_weight.shape[0]), F32),
             pltpu.VMEM((nt, part_rows, cols), F32),
@@ -325,8 +322,8 @@
             dma((5,)),
             dma((2,)), dma((2,)),
             dma((nb,)), dma((nb,)),
-            dma((2, nb)), dma((2, nb)),
-            dma((nbt,)), dma((nbt,)),
+            dma((half, nb)), dma((half, nb)),
+            dma((half, nbt)), dma((half, nbt)),
             dma((nt,)), dma((nt,)),
         ],
         compiler_params=pltpu.CompilerParams(

time: 32.5 us -> 33.2 us (1.022)
  Pallas kernels: 30.9 us -> 31.6 us
    pallas_call x1, Pallas kernels: 30.9 us -> 31.6 us  [body(): pl.pallas_call(functools.partial(kernel, nb, nbt, nt, n), out_shape=jax.S...]
where the time goes in v3:
time: 33.2 us; the launch traced here: 32.9 us
  Pallas kernels  31.6 us (95%)
  other arithmetic  1.37 us (4%)
    pallas_call x1, Pallas kernels, body(): pl.pallas_call(functools.partial(kernel, nb, nbt, nt, n), out_shape=jax.S...  31.6 us
    convert_element_type x1, other arithmetic, body(): return pl.pallas_call(functools.partial(kernel, nb, nbt, nt, n), out_shap...  1.37 us

profile of v3, /device:TPU:0, one launch (start us, length us, event | category | flops | bytes accessed | tf_op | source)
XLA Modules:
  0.0 32.9 jit_solution(13751856455733078304)
XLA Ops:
  0.0 31.6 %shard_map.91 = f32[4,2048]{1,0:T(4,128)} custom-call(bf16[4,4096]{1,0:T(4,128)(2,1)} %q_ref.1, bf16[4,512]{1,0:T(4,128)(2,1)} %nk_ref.1, bf16[4,512]{1,0:T(4,128)(2,1)} %nv_ref.1, s32[4]{0:T(128)} %len_ref.1, bf16[4,512,512]{2,1,0:T(8,128)(2,1)} %sk_hbm.1, bf16[4,512,512]{2,1,0:T(8,128)(2,1)} %sv_hbm.1, bf16[2048,512]{1,0:T(8,128)(2,1)} %pk_hbm.1, ...), custom_call_target="tpu_custom_call" | custom-call | flops 1207959552 | bytes 25165824 | tf_op jit(solution)/shard_map/pallas_call | solution.py:295
  31.6 1.4 %convert_element_type.3 = bf16[4,2048]{1,0:T(4,128)(2,1)} convert(f32[4,2048]{1,0:T(4,128)} %shard_map.91) | non-fusion elementwise | flops 8192 | bytes 49152 | tf_op jit(solution)/shard_map/convert_element_type | solution.py:338

commit v4 on v3

--- a/solution.py
+++ b/solution.py
@@ -239,11 +239,15 @@
         join(k)
         for r in range(1, nbt):
             a_copy(k, r, mb).start()
-        for r in range(1, nbt):
-            a_copy(k, r, lax.rem(mb + nbt - r, nbt)).wait_recv()
-        if k == 0:
-            loads[4].wait()
-        project(k)
+        if k > 0:
+            for r in range(1, nbt):
+                a_copy(k - 1, r, lax.rem(mb + nbt - r, nbt)).wait_recv()
+            if k == 1:
+                loads[4].wait()
+            project(k - 1)
+    for r in range(1, nbt):
+        a_copy(half - 1, r, lax.rem(mb + nbt - r, nbt)).wait_recv()
+    project(half - 1)
 
     def o_copy(r, slot):
         dst = lax.rem(mt + r, nt)

time: 33.2 us -> 31 us (0.934)
  Pallas kernels: 31.6 us -> 29.3 us
    pallas_call x1, Pallas kernels: 31.6 us -> 29.3 us  [body(): pl.pallas_call(functools.partial(kernel, nb, nbt, nt, n), out_shape=jax.S...]
where the time goes in v4:
time: 31 us; the launch traced here: 30.7 us
  Pallas kernels  29.3 us (95%)
  other arithmetic  1.37 us (4%)
    pallas_call x1, Pallas kernels, body(): pl.pallas_call(functools.partial(kernel, nb, nbt, nt, n), out_shape=jax.S...  29.3 us
    convert_element_type x1, other arithmetic, body(): return pl.pallas_call(functools.partial(kernel, nb, nbt, nt, n), out_shap...  1.37 us

profile of v4, /device:TPU:0, one launch (start us, length us, event | category | flops | bytes accessed | tf_op | source)
XLA Modules:
  0.0 30.7 jit_solution(9513213261900540334)
XLA Ops:
  0.0 29.3 %shard_map.91 = f32[4,2048]{1,0:T(4,128)} custom-call(bf16[4,4096]{1,0:T(4,128)(2,1)} %q_ref.1, bf16[4,512]{1,0:T(4,128)(2,1)} %nk_ref.1, bf16[4,512]{1,0:T(4,128)(2,1)} %nv_ref.1, s32[4]{0:T(128)} %len_ref.1, bf16[4,512,512]{2,1,0:T(8,128)(2,1)} %sk_hbm.1, bf16[4,512,512]{2,1,0:T(8,128)(2,1)} %sv_hbm.1, bf16[2048,512]{1,0:T(8,128)(2,1)} %pk_hbm.1, ...), custom_call_target="tpu_custom_call" | custom-call | flops 1207959552 | bytes 25165824 | tf_op jit(solution)/shard_map/pallas_call | solution.py:299
  29.3 1.4 %convert_element_type.3 = bf16[4,2048]{1,0:T(4,128)(2,1)} convert(f32[4,2048]{1,0:T(4,128)} %shard_map.91) | non-fusion elementwise | flops 8192 | bytes 49152 | tf_op jit(solution)/shard_map/convert_element_type | solution.py:342
